TPU v7x, 256 devices: a whole 4x4x8 slice. The times are simulated.
256 devices in a mesh: sect: 2 (over core), blk: 128 (over x, z, y).
Axes of the slice: x: 4, y: 4, z: 8, core: 2. Of those that a mesh axis runs over, the one named last changes fastest.
Arguments:
- start_remainders: bfloat16 [2, 128, 256, 256], P(None, 'blk'), may hold values from -6 to 6
- site_tensors: bfloat16 [4, 128, 4, 256, 256], P('sect', 'blk'), may hold values from -0.375 to 0.375
- mpo_coeffs: float32 [4, 4], P('sect'), may hold values from 0.25 to 2
- mpo_pattern: int32 [4, 4], P('sect'), may hold values 0 or 1
- joining: int32 [4, 4, 128], P('sect'), may hold values from 0 to 127, each once within a row
- sector_dims: int32 [4, 128], P('sect'), may hold values from 64 to 256, as said below
Outputs:
- segment_remainders: bfloat16 [2, 2, 128, 256, 256], P('sect', None, 'blk')
Inputs may be any that keep to these rules, and one draw needn't show every extreme that they name: Every joining[k, s] is a permutation of the 128 sectors. `sector_dims`: at every site some sector has the full size 256.
All inputs are finite; a program needn't handle non-finite values. No bound on the sum of `mpo_pattern` on one device may be relied on, other than what follows from the above.
Results may differ from a plain program's by a relative error of at most 0.009.
Values may be sent and summed in bfloat16 or wider, within the bound.
A program may use at most 64 MiB of HBM per device.

v0:
```python
import jax
import jax.numpy as jnp
from jax import lax
from jax.experimental import pallas as pl
from jax.experimental.pallas import tpu as pltpu
from jax.sharding import PartitionSpec as P

MESH = pl.DeviceIdType.MESH
B = 256
PHYS = 4
SITES = 4
CHIPS = 128
TILES = 64
ROWS, COLS = 8, 128
OFFSETS = [(i, j) for i in (2, 1, 3, 0) for j in (2, 1, 3, 0)]


def far_first(step):
    half, sign = (step + 1) // 2, 1 - 2 * (step % 2)
    return (12 + sign * half) % 8


def kernel(
    start_ref, tensor_ref, coeff_ref, pattern_ref, joining_ref, dims_ref, out_ref,
    coeffs, pattern, joining, tables, weights_all, lookup,
    tensors, remainder, parting, made, gathered_even, gathered_odd, joined, returned,
    tensor_sems, made_send, made_recv, joined_send, joined_recv, own_sem, part_sems, table_sems, small_sems,
):
    me, state = lax.axis_index("blk"), lax.axis_index("sect")
    x, z, y = me // 32, (me // 4) % 8, me % 4
    sibling = {"sect": 1 - state}
    tile = (x * 4 + z % 4) * 4 + y
    half = z // 4
    xs = [(x + i) % 4 for i in range(4)]
    ys = [(y + i) % 4 for i in range(4)]

    def each_chip(visit):
        def body(step, carry):
            base = ((z + far_first(step)) % 8) * 4
            for i, j in OFFSETS:
                visit(base + xs[i] * 32 + ys[j], i == 0 and j == 0)
            return carry

        lax.fori_loop(0, 8, body, 0)

    def each_hub(visit):
        for i, j in OFFSETS:
            hub_z = (z + 2 + 4 * ((xs[i] + ys[j]) % 2)) % 8
            visit(xs[i], hub_z, ys[j], False)

        def body(step, carry):
            hub_z = (z + 7 + (step + 1) % 3) % 8
            for i, j in OFFSETS:
                visit(xs[i], hub_z, ys[j], i == 0 and j == 0)
            return carry

        lax.fori_loop(1, 4, body, 0)

    def unless_me(chip, maybe_me, go):
        if maybe_me:
            pl.when(chip != me)(go)
        else:
            go()

    barrier = pltpu.get_barrier_semaphore()
    pl.semaphore_signal(barrier, inc=1, device_id=sibling, device_id_type=MESH)

    def greet(chip, maybe_me):
        unless_me(
            chip, maybe_me,
            lambda: pl.semaphore_signal(barrier, inc=1, device_id={"blk": chip}, device_id_type=MESH),
        )

    each_chip(greet)

    start_copy = pltpu.make_async_copy(start_ref.at[state], remainder, own_sem.at[1])
    start_copy.start()

    def own_tensor(j):
        return pltpu.make_async_copy(tensor_ref.at[j], tensors.at[state * 2 + j], tensor_sems.at[0, j])

    def sent_tensor(j, slot):
        return pltpu.make_async_remote_copy(
            tensor_ref.at[j], tensors.at[slot * 2 + j], tensor_sems.at[1, j], tensor_sems.at[2, j],
            device_id=sibling, device_id_type=MESH,
        )

    for j in range(2):
        own_tensor(j).start()
    small_copies = [
        pltpu.make_async_copy(source, target, small_sems.at[i])
        for i, (source, target) in enumerate(
            [
                (joining_ref, joining),
                (dims_ref, tables.at[state, pl.ds(2 * PHYS, 2)]),
                (coeff_ref, coeffs),
                (pattern_ref, pattern),
            ]
        )
    ]
    for copy in small_copies:
        copy.start()

    for i in range(4):
        away = (z + 3 + i) % 8 if i < 3 else (z + 2 + 4 * ((x + y + 1) % 2) + 4) % 8
        for column in range(4):
            slots = pl.ds(column * 32 + away * 4, 4)
            gathered_even[slots] = jnp.zeros((4, PHYS, ROWS, COLS), jnp.bfloat16)
            gathered_odd[slots] = jnp.zeros((4, PHYS, ROWS, COLS), jnp.bfloat16)

    for copy in small_copies:
        copy.wait()

    turned = jnp.concatenate([joining[...], jnp.zeros((CHIPS - 2 * PHYS, CHIPS), jnp.int32)], axis=0).T
    left_ids = lax.broadcasted_iota(jnp.int32, (CHIPS, CHIPS), 0)
    right_ids = lax.broadcasted_iota(jnp.int32, (CHIPS, CHIPS), 1)
    for row in range(2 * PHYS):
        hit = jnp.where(turned[:, row : row + 1] == right_ids, left_ids, 0)
        tables[state, row : row + 1] = jnp.max(hit, axis=0, keepdims=True)
    weights_all[state, :, :PHYS] = coeffs[...] * pattern[...].astype(jnp.float32)

    def sent_table(slot):
        return pltpu.make_async_remote_copy(
            tables.at[slot], tables.at[slot], table_sems.at[0], table_sems.at[1],
            device_id=sibling, device_id_type=MESH,
        )

    def sent_weights(slot):
        return pltpu.make_async_remote_copy(
            weights_all.at[slot], weights_all.at[slot], table_sems.at[2], table_sems.at[3],
            device_id=sibling, device_id_type=MESH,
        )

    lookup_copy = pltpu.make_async_copy(tables, lookup, table_sems.at[4])
    start_copy.wait()
    pl.semaphore_wait(barrier, CHIPS)

    for j in range(2):
        sent_tensor(j, state).start()
    sent_table(state).start()
    sent_weights(state).start()

    row_ids = (tile // 2) * ROWS + lax.broadcasted_iota(jnp.int32, (ROWS, COLS), 0)
    col_ids = (tile % 2) * COLS + lax.broadcasted_iota(jnp.int32, (ROWS, COLS), 1)

    def all_made(site):
        slots = pl.ds(0, TILES - 1)
        return pltpu.make_async_remote_copy(
            gathered_even.at[slots], gathered_even.at[slots], made_send.at[site], made_recv.at[site],
            device_id=sibling, device_id_type=MESH,
        )

    def all_joined(site):
        slots = pl.ds(0, CHIPS - 1)
        return pltpu.make_async_remote_copy(
            joined.at[site, slots], joined.at[site, slots], joined_send.at[site], joined_recv.at[site],
            device_id=sibling, device_id_type=MESH,
        )

    def part_copy(slot):
        return pltpu.make_async_remote_copy(
            parting, out_ref.at[slot], part_sems.at[0], part_sems.at[1],
            device_id=sibling, device_id_type=MESH,
        )

    def site_step(section, row, gathered):
        site = section * 2 + row

        @pl.when(section == state)
        def _():
            own_tensor(row).wait()

        @pl.when(section != state)
        def _():
            sent_tensor(row, 1 - state).wait_recv()

        for phys in range(PHYS):
            product = jnp.dot(remainder[...], tensors[site, phys], preferred_element_type=jnp.float32)
            for side in range(2):
                part = product[:, side * COLS : (side + 1) * COLS].reshape(B // ROWS, ROWS, COLS)
                made[site, :, side, phys] = part.astype(jnp.bfloat16)

        def send_made(hub_x, hub_z, hub_y, maybe_me):
            chip = hub_x * 32 + hub_z * 4 + hub_y
            there = (hub_x * 4 + hub_z % 4) * 4 + hub_y

            def go():
                pltpu.make_async_remote_copy(
                    made.at[site, there // 2, there % 2], gathered.at[me],
                    made_send.at[site], made_recv.at[site],
                    device_id={"blk": chip}, device_id_type=MESH,
                ).start()

            unless_me(chip, maybe_me, go)

        each_hub(send_made)
        own = pltpu.make_async_copy(made.at[site, tile // 2, tile % 2], gathered.at[me], own_sem.at[0])
        own.start()

        if row == 0:
            @pl.when(section == 0)
            def _():
                sent_table(1 - state).wait_recv()
                sent_weights(1 - state).wait_recv()
                lookup_copy.start()
                lookup_copy.wait()

        own.wait()
        all_made(site).wait_recv()
        weight_row = weights_all[section, row : row + 1]
        weights = [weight_row[:, phys : phys + 1] for phys in range(PHYS)]

        def join(chip, maybe_me):
            total = jnp.zeros((ROWS, COLS), jnp.float32)
            for phys in range(PHYS):
                left = lookup[section, row * PHYS + phys, chip]
                total = total + weights[phys] * gathered[left, phys].astype(jnp.float32)
            size = lookup[section, 2 * PHYS + row, chip]
            total = jnp.where((row_ids < size) & (col_ids < size), total, 0.0)
            joined[site, chip] = total.astype(jnp.bfloat16)

            def go():
                pltpu.make_async_remote_copy(
                    joined.at[site, chip], returned.at[site, half, tile],
                    joined_send.at[site], joined_recv.at[site],
                    device_id={"blk": chip}, device_id_type=MESH,
                ).start()

            unless_me(chip, maybe_me, go)

        each_chip(join)
        own = pltpu.make_async_copy(joined.at[site, me], returned.at[site, half, tile], own_sem.at[0])
        own.start()
        own.wait()
        all_joined(site).wait_recv()

        tiles = returned[site, 0].astype(jnp.float32) + returned[site, 1].astype(jnp.float32)
        squares = jnp.sum(tiles * tiles, axis=0)
        meansq = jnp.sum(squares, keepdims=True) * (1.0 / (B * B))
        scale = lax.rsqrt(meansq + 1e-06)
        tiles = (tiles * scale[None]).reshape(B // ROWS, 2, ROWS, COLS)
        for side in range(2):
            remainder[:, side * COLS : (side + 1) * COLS] = tiles[:, side].reshape(B, COLS).astype(jnp.bfloat16)

        if row == 1:
            @pl.when(section == state)
            def _():
                out_ref[state] = remainder[...]

            @pl.when(section != state)
            def _():
                parting[...] = remainder[...]
                part_copy(state).start()

    def section_step(section, carry):
        site_step(section, 0, gathered_even)
        site_step(section, 1, gathered_odd)
        return carry

    lax.fori_loop(0, SITES // 2, section_step, 0)

    for j in range(2):
        sent_tensor(j, state).wait_send()
    sent_table(state).wait_send()
    sent_weights(state).wait_send()

    def settle(site, carry):
        all_made(site).wait_send()
        all_joined(site).wait_send()
        return carry

    lax.fori_loop(0, SITES, settle, 0)
    part_copy(state).wait_send()
    part_copy(1 - state).wait_recv()


def shards(start_remainders, site_tensors, mpo_coeffs, mpo_pattern, joining, sector_dims):
    bf16, dma = jnp.bfloat16, pltpu.SemaphoreType.DMA
    out = pl.pallas_call(
        kernel,
        out_shape=jax.ShapeDtypeStruct((2, B, B), bf16),
        in_specs=[pl.BlockSpec(memory_space=pltpu.HBM)] * 6,
        out_specs=pl.BlockSpec(memory_space=pltpu.VMEM),
        scratch_shapes=[
            pltpu.VMEM((2, PHYS), jnp.float32),
            pltpu.VMEM((2, PHYS), jnp.int32),
            pltpu.VMEM((2 * PHYS, CHIPS), jnp.int32),
            pltpu.VMEM((2, 16, CHIPS), jnp.int32),
            pltpu.VMEM((2, 2, CHIPS), jnp.float32),
            pltpu.SMEM((2, 16, CHIPS), jnp.int32),
            pltpu.VMEM((SITES, PHYS, B, B), bf16),
            pltpu.VMEM((B, B), bf16),
            pltpu.VMEM((B, B), bf16),
            pltpu.VMEM((SITES, B // ROWS, 2, PHYS, ROWS, COLS), bf16),
            pltpu.VMEM((CHIPS, PHYS, ROWS, COLS), bf16),
            pltpu.VMEM((CHIPS, PHYS, ROWS, COLS), bf16),
            pltpu.VMEM((SITES, CHIPS, ROWS, COLS), bf16),
            pltpu.VMEM((SITES, 2, TILES, ROWS, COLS), bf16),
            dma((3, 2)),
            dma((SITES,)),
            dma((SITES,)),
            dma((SITES,)),
            dma((SITES,)),
            dma((2,)),
            dma((2,)),
            dma((5,)),
            dma((4,)),
        ],
        compiler_params=pltpu.CompilerParams(
            collective_id=0, has_side_effects=True, vmem_limit_bytes=63 << 20
        ),
        name="zip_up",
    )(
        start_remainders[:, 0],
        site_tensors[:, 0],
        mpo_coeffs,
        mpo_pattern,
        joining.reshape(2 * PHYS, CHIPS),
        sector_dims,
    )
    return out[None, :, None]


def solution(mesh):
    in_specs = (
        P(None, "blk", None, None),
        P("sect", "blk", None, None, None),
        P("sect", None),
        P("sect", None),
        P("sect", None, None),
        P("sect", None),
    )
    out_specs = P("sect", None, "blk", None, None)
    return jax.shard_map(shards, mesh=mesh, in_specs=in_specs, out_specs=out_specs, check_vma=False)
```

profile of v0, /device:TPU:1, one launch (start us, length us, event | category | flops | bytes accessed | tf_op | source)
XLA Modules:
  0.0 95.4 jit_solution(13399435268253291332)
XLA Ops:
  0.0 93.7 %zip_up.1 = bf16[2,256,256]{2,1,0:T(8,128)(2,1)} custom-call(bf16[2,256,256]{2,1,0:T(8,128)(2,1)} %bitcast.8, bf16[2,4,256,256]{3,2,1,0:T(8,128)(2,1)} %bitcast.6, f32[2,4]{1,0:T(2,128)} %coeff_ref.1, s32[2,4]{1,0:T(2,128)} %pattern_ref.1, s32[8,128]{1,0:T(8,128)} %bitcast.9, s32[2,128]{1,0:T(2,128)} %dims_ref.1), custom_call_target="tpu_custom_call" | custom-call | tf_op jit(solution)/shard_map/zip_up/pallas_call | solution.py:279
  93.7 1.7 %copy.9 = bf16[1,2,1,256,256]{4,3,2,1,0:T(8,128)(2,1)} copy(bf16[1,2,1,256,256]{4,3,2,1,0:T(8,128)(2,1)} %bitcast.7) | data formatting | bytes 524288
where the time goes:
time: 95.5 us; the launch traced here: 95.4 us
  Pallas kernels  93.7 us (98%)
  local copies, waits for them, and re-layouts  1.67 us (2%)
    pallas_call x1, Pallas kernels, shards(): pl.pallas_call(kernel, out_shape=jax.ShapeDtypeStruct((2, B, B), bf16), i...  93.7 us

commit v1 on v0

--- a/solution.py
+++ b/solution.py
@@ -12,12 +12,26 @@
 CHIPS = 128
 TILES = 64
 ROWS, COLS = 8, 128
-OFFSETS = [(i, j) for i in (2, 1, 3, 0) for j in (2, 1, 3, 0)]
-
-
-def far_first(step):
-    half, sign = (step + 1) // 2, 1 - 2 * (step % 2)
-    return (12 + sign * half) % 8
+def hops(d):
+    return min(d // 32, 4 - d // 32) + min(d // 4 % 8, 8 - d // 4 % 8) + min(d % 4, 4 - d % 4)
+
+
+ORDER = sorted(range(CHIPS), key=lambda d: (-hops(d), d * 37 % CHIPS))
+NEAR = [d for d in ORDER if 0 < hops(d) <= 4]
+
+
+def nearer_hubs():
+    chosen = []
+    for d in range(CHIPS):
+        opposite = (d // 32 + 2) % 4 * 32 + (d // 4 % 8 + 4) % 8 * 4 + (d % 4 + 2) % 4
+        here, there = [(hops(e), min(e // 4 % 8, 8 - e // 4 % 8)) for e in (d, opposite)]
+        tie = here == there and d in (10, 26, 41, 59, 107, 121)
+        if here < there or tie:
+            chosen.append(d)
+    return [d for d in ORDER if d in chosen]
+
+
+HUBS = nearer_hubs()
 
 
 def kernel(
@@ -29,49 +43,20 @@
     me, state = lax.axis_index("blk"), lax.axis_index("sect")
     x, z, y = me // 32, (me // 4) % 8, me % 4
     sibling = {"sect": 1 - state}
-    tile = (x * 4 + z % 4) * 4 + y
     half = z // 4
+    tile = ((x + 2 * half) % 4 * 4 + z % 4) * 4 + (y + 2 * half) % 4
     xs = [(x + i) % 4 for i in range(4)]
+    zs = [(z + i) % 8 for i in range(8)]
     ys = [(y + i) % 4 for i in range(4)]
 
-    def each_chip(visit):
-        def body(step, carry):
-            base = ((z + far_first(step)) % 8) * 4
-            for i, j in OFFSETS:
-                visit(base + xs[i] * 32 + ys[j], i == 0 and j == 0)
-            return carry
-
-        lax.fori_loop(0, 8, body, 0)
-
-    def each_hub(visit):
-        for i, j in OFFSETS:
-            hub_z = (z + 2 + 4 * ((xs[i] + ys[j]) % 2)) % 8
-            visit(xs[i], hub_z, ys[j], False)
-
-        def body(step, carry):
-            hub_z = (z + 7 + (step + 1) % 3) % 8
-            for i, j in OFFSETS:
-                visit(xs[i], hub_z, ys[j], i == 0 and j == 0)
-            return carry
-
-        lax.fori_loop(1, 4, body, 0)
-
-    def unless_me(chip, maybe_me, go):
-        if maybe_me:
-            pl.when(chip != me)(go)
-        else:
-            go()
+    def at(d):
+        return xs[d // 32] * 32 + zs[d // 4 % 8] * 4 + ys[d % 4]
 
     barrier = pltpu.get_barrier_semaphore()
     pl.semaphore_signal(barrier, inc=1, device_id=sibling, device_id_type=MESH)
 
-    def greet(chip, maybe_me):
-        unless_me(
-            chip, maybe_me,
-            lambda: pl.semaphore_signal(barrier, inc=1, device_id={"blk": chip}, device_id_type=MESH),
-        )
-
-    each_chip(greet)
+    for d in NEAR:
+        pl.semaphore_signal(barrier, inc=1, device_id={"blk": at(d)}, device_id_type=MESH)
 
     start_copy = pltpu.make_async_copy(start_ref.at[state], remainder, own_sem.at[1])
     start_copy.start()
@@ -101,12 +86,11 @@
     for copy in small_copies:
         copy.start()
 
-    for i in range(4):
-        away = (z + 3 + i) % 8 if i < 3 else (z + 2 + 4 * ((x + y + 1) % 2) + 4) % 8
-        for column in range(4):
-            slots = pl.ds(column * 32 + away * 4, 4)
-            gathered_even[slots] = jnp.zeros((4, PHYS, ROWS, COLS), jnp.bfloat16)
-            gathered_odd[slots] = jnp.zeros((4, PHYS, ROWS, COLS), jnp.bfloat16)
+    for d in range(CHIPS):
+        if d not in HUBS:
+            slot = at((4 - d // 32) % 4 * 32 + (8 - d // 4 % 8) % 8 * 4 + (4 - d % 4) % 4)
+            gathered_even[slot] = jnp.zeros((PHYS, ROWS, COLS), jnp.bfloat16)
+            gathered_odd[slot] = jnp.zeros((PHYS, ROWS, COLS), jnp.bfloat16)
 
     for copy in small_copies:
         copy.wait()
@@ -133,7 +117,7 @@
 
     lookup_copy = pltpu.make_async_copy(tables, lookup, table_sems.at[4])
     start_copy.wait()
-    pl.semaphore_wait(barrier, CHIPS)
+    pl.semaphore_wait(barrier, len(NEAR) + 1)
 
     for j in range(2):
         sent_tensor(j, state).start()
@@ -153,13 +137,13 @@
     def all_joined(site):
         slots = pl.ds(0, CHIPS - 1)
         return pltpu.make_async_remote_copy(
-            joined.at[site, slots], joined.at[site, slots], joined_send.at[site], joined_recv.at[site],
-            device_id=sibling, device_id_type=MESH,
-        )
-
-    def part_copy(slot):
-        return pltpu.make_async_remote_copy(
-            parting, out_ref.at[slot], part_sems.at[0], part_sems.at[1],
+            joined.at[0, slots], joined.at[0, slots], joined_send.at[site], joined_recv.at[site],
+            device_id=sibling, device_id_type=MESH,
+        )
+
+    def part_copy():
+        return pltpu.make_async_remote_copy(
+            parting, out_ref.at[1], part_sems.at[0], part_sems.at[1],
             device_id=sibling, device_id_type=MESH,
         )
 
@@ -180,20 +164,15 @@
                 part = product[:, side * COLS : (side + 1) * COLS].reshape(B // ROWS, ROWS, COLS)
                 made[site, :, side, phys] = part.astype(jnp.bfloat16)
 
-        def send_made(hub_x, hub_z, hub_y, maybe_me):
-            chip = hub_x * 32 + hub_z * 4 + hub_y
-            there = (hub_x * 4 + hub_z % 4) * 4 + hub_y
-
-            def go():
+        for d in HUBS:
+            if d:
+                hub_half = zs[d // 4 % 8] // 4
+                hub_tile = ((xs[d // 32] + 2 * hub_half) % 4 * 4 + zs[d // 4 % 8] % 4) * 4 + (ys[d % 4] + 2 * hub_half) % 4
                 pltpu.make_async_remote_copy(
-                    made.at[site, there // 2, there % 2], gathered.at[me],
+                    made.at[site, hub_tile // 2, hub_tile % 2], gathered.at[me],
                     made_send.at[site], made_recv.at[site],
-                    device_id={"blk": chip}, device_id_type=MESH,
+                    device_id={"blk": at(d)}, device_id_type=MESH,
                 ).start()
-
-            unless_me(chip, maybe_me, go)
-
-        each_hub(send_made)
         own = pltpu.make_async_copy(made.at[site, tile // 2, tile % 2], gathered.at[me], own_sem.at[0])
         own.start()
 
@@ -210,7 +189,10 @@
         weight_row = weights_all[section, row : row + 1]
         weights = [weight_row[:, phys : phys + 1] for phys in range(PHYS)]
 
-        def join(chip, maybe_me):
+        crossing = (1 - state) * section * row
+        core, lane = state + crossing, site + crossing
+        for d in ORDER:
+            chip = at(d)
             total = jnp.zeros((ROWS, COLS), jnp.float32)
             for phys in range(PHYS):
                 left = lookup[section, row * PHYS + phys, chip]
@@ -218,39 +200,64 @@
             size = lookup[section, 2 * PHYS + row, chip]
             total = jnp.where((row_ids < size) & (col_ids < size), total, 0.0)
             joined[site, chip] = total.astype(jnp.bfloat16)
-
-            def go():
+            if d:
                 pltpu.make_async_remote_copy(
-                    joined.at[site, chip], returned.at[site, half, tile],
-                    joined_send.at[site], joined_recv.at[site],
-                    device_id={"blk": chip}, device_id_type=MESH,
+                    joined.at[site, chip], returned.at[site, state, half, tile],
+                    joined_send.at[lane], joined_recv.at[lane],
+                    device_id={"sect": core, "blk": chip}, device_id_type=MESH,
                 ).start()
 
-            unless_me(chip, maybe_me, go)
-
-        each_chip(join)
-        own = pltpu.make_async_copy(joined.at[site, me], returned.at[site, half, tile], own_sem.at[0])
-        own.start()
-        own.wait()
-        all_joined(site).wait_recv()
-
-        tiles = returned[site, 0].astype(jnp.float32) + returned[site, 1].astype(jnp.float32)
-        squares = jnp.sum(tiles * tiles, axis=0)
-        meansq = jnp.sum(squares, keepdims=True) * (1.0 / (B * B))
-        scale = lax.rsqrt(meansq + 1e-06)
-        tiles = (tiles * scale[None]).reshape(B // ROWS, 2, ROWS, COLS)
-        for side in range(2):
-            remainder[:, side * COLS : (side + 1) * COLS] = tiles[:, side].reshape(B, COLS).astype(jnp.bfloat16)
-
-        if row == 1:
-            @pl.when(section == state)
-            def _():
-                out_ref[state] = remainder[...]
-
-            @pl.when(section != state)
+        def finish(held):
+            tiles = returned[site, held, 0].astype(jnp.float32) + returned[site, held, 1].astype(jnp.float32)
+            squares = jnp.sum(tiles * tiles, axis=0)
+            meansq = jnp.sum(squares, keepdims=True) * (1.0 / (B * B))
+            scale = lax.rsqrt(meansq + 1e-06)
+            tiles = (tiles * scale[None]).reshape(B // ROWS, 2, ROWS, COLS)
+            for side in range(2):
+                part = tiles[:, side].reshape(B, COLS).astype(jnp.bfloat16)
+                remainder[:, side * COLS : (side + 1) * COLS] = part
+
+        def to_sibling():
+            return pltpu.make_async_remote_copy(
+                joined.at[site, me], returned.at[site, state, half, tile],
+                part_sems.at[2], part_sems.at[3], device_id=sibling, device_id_type=MESH,
+            )
+
+        def keep_own():
+            own = pltpu.make_async_copy(joined.at[site, me], returned.at[site, state, half, tile], own_sem.at[0])
+            own.start()
+            own.wait()
+            all_joined(site).wait_recv()
+            finish(state)
+
+        if row == 0:
+            keep_own()
+        else:
+            @pl.when((section == 0) | (state == 1))
+            def _():
+                keep_own()
+
+            @pl.when((section == 0) & (state == 0))
+            def _():
+                out_ref[0] = remainder[...]
+
+            @pl.when((section == 0) & (state == 1))
             def _():
                 parting[...] = remainder[...]
-                part_copy(state).start()
+                part_copy().start()
+
+            @pl.when((section == 1) & (state == 0))
+            def _():
+                to_sibling().start()
+                to_sibling().wait_send()
+
+            @pl.when((section == 1) & (state == 1))
+            def _():
+                out_ref[1] = remainder[...]
+                to_sibling().wait_recv()
+                all_joined(SITES).wait_recv()
+                finish(0)
+                out_ref[0] = remainder[...]
 
     def section_step(section, carry):
         site_step(section, 0, gathered_even)
@@ -266,12 +273,18 @@
 
     def settle(site, carry):
         all_made(site).wait_send()
-        all_joined(site).wait_send()
+        all_joined(site + (1 - state) * (site // (SITES - 1))).wait_send()
         return carry
 
     lax.fori_loop(0, SITES, settle, 0)
-    part_copy(state).wait_send()
-    part_copy(1 - state).wait_recv()
+
+    @pl.when(state == 1)
+    def _():
+        part_copy().wait_send()
+
+    @pl.when(state == 0)
+    def _():
+        part_copy().wait_recv()
 
 
 def shards(start_remainders, site_tensors, mpo_coeffs, mpo_pattern, joining, sector_dims):
@@ -295,14 +308,14 @@
             pltpu.VMEM((CHIPS, PHYS, ROWS, COLS), bf16),
             pltpu.VMEM((CHIPS, PHYS, ROWS, COLS), bf16),
             pltpu.VMEM((SITES, CHIPS, ROWS, COLS), bf16),
-            pltpu.VMEM((SITES, 2, TILES, ROWS, COLS), bf16),
+            pltpu.VMEM((SITES, 2, 2, TILES, ROWS, COLS), bf16),
             dma((3, 2)),
             dma((SITES,)),
             dma((SITES,)),
-            dma((SITES,)),
-            dma((SITES,)),
+            dma((SITES + 1,)),
+            dma((SITES + 1,)),
             dma((2,)),
-            dma((2,)),
+            dma((4,)),
             dma((5,)),
             dma((4,)),
         ],

time: 95.5 us -> 87.9 us (0.920)
  Pallas kernels: 93.7 us -> 86.1 us
    pallas_call x1, Pallas kernels: 93.7 us -> 86.1 us  [shards(): pl.pallas_call(kernel, out_shape=jax.ShapeDtypeStruct((2, B, B), bf16), i...]
where the time goes in v1:
time: 87.9 us; the launch traced here: 87.8 us
  Pallas kernels  86.1 us (98%)
  local copies, waits for them, and re-layouts  1.67 us (2%)
    pallas_call x1, Pallas kernels, shards(): pl.pallas_call(kernel, out_shape=jax.ShapeDtypeStruct((2, B, B), bf16), i...  86.1 us

profile of v1, /device:TPU:1, one launch (start us, length us, event | category | flops | bytes accessed | tf_op | source)
XLA Modules:
  0.0 87.8 jit_solution(8287733814489750310)
XLA Ops:
  0.0 86.1 %zip_up.1 = bf16[2,256,256]{2,1,0:T(8,128)(2,1)} custom-call(bf16[2,256,256]{2,1,0:T(8,128)(2,1)} %bitcast.8, bf16[2,4,256,256]{3,2,1,0:T(8,128)(2,1)} %bitcast.6, f32[2,4]{1,0:T(2,128)} %coeff_ref.1, s32[2,4]{1,0:T(2,128)} %pattern_ref.1, s32[8,128]{1,0:T(8,128)} %bitcast.9, s32[2,128]{1,0:T(2,128)} %dims_ref.1), custom_call_target="tpu_custom_call" | custom-call | tf_op jit(solution)/shard_map/zip_up/pallas_call | solution.py:292
  86.1 1.7 %copy.9 = bf16[1,2,1,256,256]{4,3,2,1,0:T(8,128)(2,1)} copy(bf16[1,2,1,256,256]{4,3,2,1,0:T(8,128)(2,1)} %bitcast.7) | data formatting | bytes 524288

commit v2 on v1

--- a/solution.py
+++ b/solution.py
@@ -16,7 +16,15 @@
     return min(d // 32, 4 - d // 32) + min(d // 4 % 8, 8 - d // 4 % 8) + min(d % 4, 4 - d % 4)
 
 
-ORDER = sorted(range(CHIPS), key=lambda d: (-hops(d), d * 37 % CHIPS))
+def alternate():
+    chosen = []
+    for d in sorted(range(CHIPS), key=lambda d: (-hops(d), d * 37 % CHIPS)):
+        back = (4 - d // 32) % 4 * 32 + (8 - d // 4 % 8) % 8 * 4 + (4 - d % 4) % 4
+        chosen += [e for e in (d, back) if e not in chosen]
+    return [e for i, e in enumerate(chosen) if e not in chosen[:i]]
+
+
+ORDER = alternate()
 NEAR = [d for d in ORDER if 0 < hops(d) <= 4]
 
 
@@ -45,9 +53,10 @@
     sibling = {"sect": 1 - state}
     half = z // 4
     tile = ((x + 2 * half) % 4 * 4 + z % 4) * 4 + (y + 2 * half) % 4
-    xs = [(x + i) % 4 for i in range(4)]
-    zs = [(z + i) % 8 for i in range(8)]
-    ys = [(y + i) % 4 for i in range(4)]
+    way = 1 - 2 * state
+    xs = [(x + 4 + way * i) % 4 for i in range(4)]
+    zs = [(z + 8 + way * i) % 8 for i in range(8)]
+    ys = [(y + 4 + way * i) % 4 for i in range(4)]
 
     def at(d):
         return xs[d // 32] * 32 + zs[d // 4 % 8] * 4 + ys[d % 4]

time: 87.9 us -> 87 us (0.990)
  Pallas kernels: 86.1 us -> 85.2 us
    pallas_call x1, Pallas kernels: 86.1 us -> 85.2 us  [shards(): pl.pallas_call(kernel, out_shape=jax.ShapeDtypeStruct((2, B, B), bf16), i...]
where the time goes in v2:
time: 87 us; the launch traced here: 86.8 us
  Pallas kernels  85.2 us (98%)
  local copies, waits for them, and re-layouts  1.67 us (2%)
    pallas_call x1, Pallas kernels, shards(): pl.pallas_call(kernel, out_shape=jax.ShapeDtypeStruct((2, B, B), bf16), i...  85.2 us

profile of v2, /device:TPU:1, one launch (start us, length us, event | category | flops | bytes accessed | tf_op | source)
XLA Modules:
  0.0 86.8 jit_solution(912176576456408360)
XLA Ops:
  0.0 85.2 %zip_up.1 = bf16[2,256,256]{2,1,0:T(8,128)(2,1)} custom-call(bf16[2,256,256]{2,1,0:T(8,128)(2,1)} %bitcast.8, bf16[2,4,256,256]{3,2,1,0:T(8,128)(2,1)} %bitcast.6, f32[2,4]{1,0:T(2,128)} %coeff_ref.1, s32[2,4]{1,0:T(2,128)} %pattern_ref.1, s32[8,128]{1,0:T(8,128)} %bitcast.9, s32[2,128]{1,0:T(2,128)} %dims_ref.1), custom_call_target="tpu_custom_call" | custom-call | tf_op jit(solution)/shard_map/zip_up/pallas_call | solution.py:301
  85.2 1.7 %copy.9 = bf16[1,2,1,256,256]{4,3,2,1,0:T(8,128)(2,1)} copy(bf16[1,2,1,256,256]{4,3,2,1,0:T(8,128)(2,1)} %bitcast.7) | data formatting | bytes 524288

commit v3 on v2

--- a/solution.py
+++ b/solution.py
@@ -18,7 +18,7 @@
 
 def alternate():
     chosen = []
-    for d in sorted(range(CHIPS), key=lambda d: (-hops(d), d * 37 % CHIPS)):
+    for d in sorted(range(CHIPS), key=lambda d: (-hops(d), d * 75 % CHIPS)):
         back = (4 - d // 32) % 4 * 32 + (8 - d // 4 % 8) % 8 * 4 + (4 - d % 4) % 4
         chosen += [e for e in (d, back) if e not in chosen]
     return [e for i, e in enumerate(chosen) if e not in chosen[:i]]

time: 87 us -> 86.5 us (level)
  no operation moved by 1% of the time
where the time goes in v3:
time: 86.5 us; the launch traced here: 86.3 us
  Pallas kernels  84.7 us (98%)
  local copies, waits for them, and re-layouts  1.67 us (2%)
    pallas_call x1, Pallas kernels, shards(): pl.pallas_call(kernel, out_shape=jax.ShapeDtypeStruct((2, B, B), bf16), i...  84.7 us

profile of v3, /device:TPU:1, one launch (start us, length us, event | category | flops | bytes accessed | tf_op | source)
XLA Modules:
  0.0 86.3 jit_solution(18290574284683943619)
XLA Ops:
  0.0 84.7 %zip_up.1 = bf16[2,256,256]{2,1,0:T(8,128)(2,1)} custom-call(bf16[2,256,256]{2,1,0:T(8,128)(2,1)} %bitcast.8, bf16[2,4,256,256]{3,2,1,0:T(8,128)(2,1)} %bitcast.6, f32[2,4]{1,0:T(2,128)} %coeff_ref.1, s32[2,4]{1,0:T(2,128)} %pattern_ref.1, s32[8,128]{1,0:T(8,128)} %bitcast.9, s32[2,128]{1,0:T(2,128)} %dims_ref.1), custom_call_target="tpu_custom_call" | custom-call | tf_op jit(solution)/shard_map/zip_up/pallas_call | solution.py:301
  84.7 1.7 %copy.9 = bf16[1,2,1,256,256]{4,3,2,1,0:T(8,128)(2,1)} copy(bf16[1,2,1,256,256]{4,3,2,1,0:T(8,128)(2,1)} %bitcast.7) | data formatting | bytes 524288
